TPU v7x, 128 devices: a whole 4x4x4 slice. The times are simulated.
128 devices in a mesh: lat: 64 (over z, y, x), lev: 2 (over core).
Axes of the slice: x: 4, y: 4, z: 4, core: 2. Of those that a mesh axis runs over, the one named last changes fastest.
Arguments:
- grid_values: bfloat16 [2560, 64, 5136], P('lat', 'lev'), may hold values from -6 to 6
- lat_counts: int32 [1280], P('lat'), may hold values from 8 to 5136, as said below
- wave_table: int32 [128], replicated, may hold values from 0 to 1279, as said below
- inverses: float32 [2560, 2, 32, 32], P('lat'), may hold values from -1 to 1
- legendre: bfloat16 [128, 2, 640, 1280], P('lat', None, 'lev')
Outputs:
- spectral: bfloat16 [128, 2, 640, 128], P('lat', None, 'lev')
Inputs may be any that keep to these rules, and one draw needn't show every extreme that they name: `lat_counts`: a multiple of 4 on every pair; 8 on the polar pair, 5136 on the pair nearest the equator, 20 + 4 p less 0 to 12 on pair p between. `wave_table`: distinct wavenumbers; 0 and 1279 are always among them.
All inputs are finite; a program needn't handle non-finite values.
Results may differ from a plain program's by a relative error of at most 0.015.
Values may be sent and summed in bfloat16 or wider, within the bound.
No kernel may reach another device: no remote copies, remote signals or barrier semaphores. Data moves between devices by JAX's collectives and lax.ppermute only.
A program may use at most 128 MiB of HBM per device.

v0:
```python
import math
import jax
import jax.numpy as jnp
from jax import lax
from jax.sharding import PartitionSpec as P

TRUNC = 1279


def fourier_table(point_count, wavenumbers, width):
    positions = jnp.arange(width, dtype=jnp.int32)
    phase_index = positions[:, None] * wavenumbers[None, :] % point_count
    angles = phase_index.astype(jnp.float32) * (2.0 * math.pi) / point_count.astype(jnp.float32)
    inside = (positions < point_count)[:, None]
    cosines = jnp.where(inside, jnp.cos(angles), 0.0)
    sines = jnp.where(inside, -jnp.sin(angles), 0.0)
    return jnp.concatenate([cosines, sines], axis=1).astype(jnp.bfloat16)


def mix_levels(fourier, inverses):
    band = fourier.shape[0]
    fields = inverses.shape[1]
    levels = inverses.shape[2]
    slots = fourier.shape[3]
    split_data = fourier.astype(jnp.float32).reshape(band, levels, fields, 2, slots)
    mixed = jnp.einsum("aflk,akfrs->sarlf", inverses, split_data, precision=lax.Precision.HIGHEST)
    return mixed.reshape(slots, band, 2, levels * fields)


def fold_pairs(owned):
    wave_count = owned.shape[0]
    all_lats = owned.shape[1]
    columns = owned.shape[3]
    paired = owned.reshape(wave_count, all_lats // 2, 2, 2 * columns)
    return jnp.stack(
        [paired[:, :, 0] + paired[:, :, 1], paired[:, :, 0] - paired[:, :, 1]], axis=1
    ).astype(jnp.bfloat16)


def on_device(grid_values, lat_counts, wave_table, inverses, legendre):
    pair_total = lat_counts.shape[0]
    slab_width = grid_values.shape[1]
    slot_total = wave_table.shape[0]
    storage = grid_values.shape[2]
    grouped = grid_values.reshape(pair_total, 2 * slab_width, storage)

    def transform(item):
        pair_rows, point_count = item
        basis = fourier_table(point_count, wave_table, storage)
        product = jnp.dot(pair_rows, basis, preferred_element_type=jnp.float32)
        product = product / point_count.astype(jnp.float32)
        return product.astype(jnp.bfloat16).reshape(2, slab_width, 2, slot_total)

    fourier = lax.map(transform, (grouped, lat_counts)).reshape(
        2 * pair_total, slab_width, 2, slot_total
    )
    every_level = lax.all_gather(fourier, "lev", axis=1, tiled=True)
    mixed_band = mix_levels(every_level, inverses)
    own_slab = lax.dynamic_slice_in_dim(
        mixed_band, lax.axis_index("lev") * slab_width, slab_width, 3
    )
    slab_owned = lax.all_to_all(
        own_slab.astype(jnp.bfloat16), "lat", split_axis=0, concat_axis=1, tiled=True
    ).astype(own_slab.dtype)
    owned = lax.all_gather(slab_owned.astype(jnp.bfloat16), "lev", axis=3, tiled=True).astype(
        slab_owned.dtype
    )
    folded = fold_pairs(owned)
    wave_count = folded.shape[0]
    summed = jnp.einsum("wqjp,wqpe->wqje", legendre, folded, preferred_element_type=jnp.float32)
    degree_rows = legendre.shape[2]
    wavenumbers = lax.dynamic_slice_in_dim(
        wave_table, lax.axis_index("lat") * wave_count, wave_count
    )
    steps_index = lax.axis_index("lev") * degree_rows + jnp.arange(degree_rows, dtype=jnp.int32)
    parity = jnp.arange(2, dtype=jnp.int32)
    degree = wavenumbers[:, None, None] + 2 * steps_index[None, None, :] + parity[None, :, None]
    keep = (degree <= TRUNC)[:, :, :, None]
    return jnp.where(keep, summed, 0.0).astype(jnp.bfloat16)


def solution(mesh):
    placed = (
        P("lat", "lev", None),
        P("lat"),
        P(),
        P("lat", None, None, None),
        P("lat", None, "lev", None),
    )
    return jax.shard_map(
        on_device,
        mesh=mesh,
        in_specs=placed,
        out_specs=P("lat", None, "lev", None),
        check_vma=False,
    )
```

profile of v0, /device:TPU:1, one launch (start us, length us, event | category | flops | bytes accessed | tf_op | source)
XLA Modules:
  0.0 989.2 jit_solution(5237779508937216669)
XLA Ops:
  6.5 875.8 %while.10 = (s32[]{:T(128)}, bf16[20,2,32,2,128]{4,1,0,3,2:T(2,128)(2,1)}, bf16[20,64,5136]{2,1,0:T(8,128)(2,1)}, s32[20]{0:T(128)}, s32[128]{0:T(128)}, /*index=5*/s32[]{:T(128)}, s32[]{:T(128)}) while((s32[]{:T(128)}, bf16[20,2,32,2,128]{4,1,0,3,2:T(2,128)(2,1)}, bf16[20,64,5136]{2,1,0:T(8,128)(2,1)}, s32[20]{0:T(128)}, s32[128]{0:T(128)}, ...), condition=%wide.region_1.2_spmd, body=%wide.region_0.1_spmd.sunk | while | flops 184112144 | bytes 6106801 | solution.py:54
  10.5 37.6 %select_convert_fusion.3 = (bf16[5136,128]{1,0:T(8,128)(2,1)S(1)}, bf16[5136,128]{1,0:T(8,128)(2,1)S(1)}) fusion(pred[5136]{0:T(1024)(128)(4,1)S(1)} %iota_compare_fusion.2, f32[]{:T(128)S(6)} %convert_element_type.47, pred[]{:T(512)S(6)} %lt.50, s32[]{:T(128)S(6)} %select_n.53, s32[128]{0:T(128)} %get-tuple-element.102), kind=kLoop, calls=%fused_computation.9.clone.1 | loop fusion | flops 10518528 | bytes 2635289 | tf_op jit(solution)/shard_map/convert
  54.3 37.6 %select_convert_fusion.3 = (bf16[5136,128]{1,0:T(8,128)(2,1)S(1)}, bf16[5136,128]{1,0:T(8,128)(2,1)S(1)}) fusion(pred[5136]{0:T(1024)(128)(4,1)S(1)} %iota_compare_fusion.2, f32[]{:T(128)S(6)} %convert_element_type.47, pred[]{:T(512)S(6)} %lt.50, s32[]{:T(128)S(6)} %select_n.53, s32[128]{0:T(128)} %get-tuple-element.102), kind=kLoop, calls=%fused_computation.9.clone.1 | loop fusion | flops 10518528 | bytes 2635289 | tf_op jit(solution)/shard_map/convert
  98.1 37.6 %select_convert_fusion.3 = (bf16[5136,128]{1,0:T(8,128)(2,1)S(1)}, bf16[5136,128]{1,0:T(8,128)(2,1)S(1)}) fusion(pred[5136]{0:T(1024)(128)(4,1)S(1)} %iota_compare_fusion.2, f32[]{:T(128)S(6)} %convert_element_type.47, pred[]{:T(512)S(6)} %lt.50, s32[]{:T(128)S(6)} %select_n.53, s32[128]{0:T(128)} %get-tuple-element.102), kind=kLoop, calls=%fused_computation.9.clone.1 | loop fusion | flops 10518528 | bytes 2635289 | tf_op jit(solution)/shard_map/convert
  141.9 37.6 %select_convert_fusion.3 = (bf16[5136,128]{1,0:T(8,128)(2,1)S(1)}, bf16[5136,128]{1,0:T(8,128)(2,1)S(1)}) fusion(pred[5136]{0:T(1024)(128)(4,1)S(1)} %iota_compare_fusion.2, f32[]{:T(128)S(6)} %convert_element_type.47, pred[]{:T(512)S(6)} %lt.50, s32[]{:T(128)S(6)} %select_n.53, s32[128]{0:T(128)} %get-tuple-element.102), kind=kLoop, calls=%fused_computation.9.clone.1 | loop fusion | flops 10518528 | bytes 2635289 | tf_op jit(solution)/shard_map/convert
  185.6 37.6 %select_convert_fusion.3 = (bf16[5136,128]{1,0:T(8,128)(2,1)S(1)}, bf16[5136,128]{1,0:T(8,128)(2,1)S(1)}) fusion(pred[5136]{0:T(1024)(128)(4,1)S(1)} %iota_compare_fusion.2, f32[]{:T(128)S(6)} %convert_element_type.47, pred[]{:T(512)S(6)} %lt.50, s32[]{:T(128)S(6)} %select_n.53, s32[128]{0:T(128)} %get-tuple-element.102), kind=kLoop, calls=%fused_computation.9.clone.1 | loop fusion | flops 10518528 | bytes 2635289 | tf_op jit(solution)/shard_map/convert
  229.4 37.6 %select_convert_fusion.3 = (bf16[5136,128]{1,0:T(8,128)(2,1)S(1)}, bf16[5136,128]{1,0:T(8,128)(2,1)S(1)}) fusion(pred[5136]{0:T(1024)(128)(4,1)S(1)} %iota_compare_fusion.2, f32[]{:T(128)S(6)} %convert_element_type.47, pred[]{:T(512)S(6)} %lt.50, s32[]{:T(128)S(6)} %select_n.53, s32[128]{0:T(128)} %get-tuple-element.102), kind=kLoop, calls=%fused_computation.9.clone.1 | loop fusion | flops 10518528 | bytes 2635289 | tf_op jit(solution)/shard_map/convert
  273.2 37.6 %select_convert_fusion.3 = (bf16[5136,128]{1,0:T(8,128)(2,1)S(1)}, bf16[5136,128]{1,0:T(8,128)(2,1)S(1)}) fusion(pred[5136]{0:T(1024)(128)(4,1)S(1)} %iota_compare_fusion.2, f32[]{:T(128)S(6)} %convert_element_type.47, pred[]{:T(512)S(6)} %lt.50, s32[]{:T(128)S(6)} %select_n.53, s32[128]{0:T(128)} %get-tuple-element.102), kind=kLoop, calls=%fused_computation.9.clone.1 | loop fusion | flops 10518528 | bytes 2635289 | tf_op jit(solution)/shard_map/convert
  317.0 37.6 %select_convert_fusion.3 = (bf16[5136,128]{1,0:T(8,128)(2,1)S(1)}, bf16[5136,128]{1,0:T(8,128)(2,1)S(1)}) fusion(pred[5136]{0:T(1024)(128)(4,1)S(1)} %iota_compare_fusion.2, f32[]{:T(128)S(6)} %convert_element_type.47, pred[]{:T(512)S(6)} %lt.50, s32[]{:T(128)S(6)} %select_n.53, s32[128]{0:T(128)} %get-tuple-element.102), kind=kLoop, calls=%fused_computation.9.clone.1 | loop fusion | flops 10518528 | bytes 2635289 | tf_op jit(solution)/shard_map/convert
  360.7 37.6 %select_convert_fusion.3 = (bf16[5136,128]{1,0:T(8,128)(2,1)S(1)}, bf16[5136,128]{1,0:T(8,128)(2,1)S(1)}) fusion(pred[5136]{0:T(1024)(128)(4,1)S(1)} %iota_compare_fusion.2, f32[]{:T(128)S(6)} %convert_element_type.47, pred[]{:T(512)S(6)} %lt.50, s32[]{:T(128)S(6)} %select_n.53, s32[128]{0:T(128)} %get-tuple-element.102), kind=kLoop, calls=%fused_computation.9.clone.1 | loop fusion | flops 10518528 | bytes 2635289 | tf_op jit(solution)/shard_map/convert
  404.5 37.6 %select_convert_fusion.3 = (bf16[5136,128]{1,0:T(8,128)(2,1)S(1)}, bf16[5136,128]{1,0:T(8,128)(2,1)S(1)}) fusion(pred[5136]{0:T(1024)(128)(4,1)S(1)} %iota_compare_fusion.2, f32[]{:T(128)S(6)} %convert_element_type.47, pred[]{:T(512)S(6)} %lt.50, s32[]{:T(128)S(6)} %select_n.53, s32[128]{0:T(128)} %get-tuple-element.102), kind=kLoop, calls=%fused_computation.9.clone.1 | loop fusion | flops 10518528 | bytes 2635289 | tf_op jit(solution)/shard_map/convert
  448.3 37.6 %select_convert_fusion.3 = (bf16[5136,128]{1,0:T(8,128)(2,1)S(1)}, bf16[5136,128]{1,0:T(8,128)(2,1)S(1)}) fusion(pred[5136]{0:T(1024)(128)(4,1)S(1)} %iota_compare_fusion.2, f32[]{:T(128)S(6)} %convert_element_type.47, pred[]{:T(512)S(6)} %lt.50, s32[]{:T(128)S(6)} %select_n.53, s32[128]{0:T(128)} %get-tuple-element.102), kind=kLoop, calls=%fused_computation.9.clone.1 | loop fusion | flops 10518528 | bytes 2635289 | tf_op jit(solution)/shard_map/convert
  492.1 37.6 %select_convert_fusion.3 = (bf16[5136,128]{1,0:T(8,128)(2,1)S(1)}, bf16[5136,128]{1,0:T(8,128)(2,1)S(1)}) fusion(pred[5136]{0:T(1024)(128)(4,1)S(1)} %iota_compare_fusion.2, f32[]{:T(128)S(6)} %convert_element_type.47, pred[]{:T(512)S(6)} %lt.50, s32[]{:T(128)S(6)} %select_n.53, s32[128]{0:T(128)} %get-tuple-element.102), kind=kLoop, calls=%fused_computation.9.clone.1 | loop fusion | flops 10518528 | bytes 2635289 | tf_op jit(solution)/shard_map/convert
  535.9 37.6 %select_convert_fusion.3 = (bf16[5136,128]{1,0:T(8,128)(2,1)S(1)}, bf16[5136,128]{1,0:T(8,128)(2,1)S(1)}) fusion(pred[5136]{0:T(1024)(128)(4,1)S(1)} %iota_compare_fusion.2, f32[]{:T(128)S(6)} %convert_element_type.47, pred[]{:T(512)S(6)} %lt.50, s32[]{:T(128)S(6)} %select_n.53, s32[128]{0:T(128)} %get-tuple-element.102), kind=kLoop, calls=%fused_computation.9.clone.1 | loop fusion | flops 10518528 | bytes 2635289 | tf_op jit(solution)/shard_map/convert
  579.7 37.6 %select_convert_fusion.3 = (bf16[5136,128]{1,0:T(8,128)(2,1)S(1)}, bf16[5136,128]{1,0:T(8,128)(2,1)S(1)}) fusion(pred[5136]{0:T(1024)(128)(4,1)S(1)} %iota_compare_fusion.2, f32[]{:T(128)S(6)} %convert_element_type.47, pred[]{:T(512)S(6)} %lt.50, s32[]{:T(128)S(6)} %select_n.53, s32[128]{0:T(128)} %get-tuple-element.102), kind=kLoop, calls=%fused_computation.9.clone.1 | loop fusion | flops 10518528 | bytes 2635289 | tf_op jit(solution)/shard_map/convert
  623.5 37.6 %select_convert_fusion.3 = (bf16[5136,128]{1,0:T(8,128)(2,1)S(1)}, bf16[5136,128]{1,0:T(8,128)(2,1)S(1)}) fusion(pred[5136]{0:T(1024)(128)(4,1)S(1)} %iota_compare_fusion.2, f32[]{:T(128)S(6)} %convert_element_type.47, pred[]{:T(512)S(6)} %lt.50, s32[]{:T(128)S(6)} %select_n.53, s32[128]{0:T(128)} %get-tuple-element.102), kind=kLoop, calls=%fused_computation.9.clone.1 | loop fusion | flops 10518528 | bytes 2635289 | tf_op jit(solution)/shard_map/convert
  667.3 37.6 %select_convert_fusion.3 = (bf16[5136,128]{1,0:T(8,128)(2,1)S(1)}, bf16[5136,128]{1,0:T(8,128)(2,1)S(1)}) fusion(pred[5136]{0:T(1024)(128)(4,1)S(1)} %iota_compare_fusion.2, f32[]{:T(128)S(6)} %convert_element_type.47, pred[]{:T(512)S(6)} %lt.50, s32[]{:T(128)S(6)} %select_n.53, s32[128]{0:T(128)} %get-tuple-element.102), kind=kLoop, calls=%fused_computation.9.clone.1 | loop fusion | flops 10518528 | bytes 2635289 | tf_op jit(solution)/shard_map/convert
  711.1 37.6 %select_convert_fusion.3 = (bf16[5136,128]{1,0:T(8,128)(2,1)S(1)}, bf16[5136,128]{1,0:T(8,128)(2,1)S(1)}) fusion(pred[5136]{0:T(1024)(128)(4,1)S(1)} %iota_compare_fusion.2, f32[]{:T(128)S(6)} %convert_element_type.47, pred[]{:T(512)S(6)} %lt.50, s32[]{:T(128)S(6)} %select_n.53, s32[128]{0:T(128)} %get-tuple-element.102), kind=kLoop, calls=%fused_computation.9.clone.1 | loop fusion | flops 10518528 | bytes 2635289 | tf_op jit(solution)/shard_map/convert
  754.8 37.6 %select_convert_fusion.3 = (bf16[5136,128]{1,0:T(8,128)(2,1)S(1)}, bf16[5136,128]{1,0:T(8,128)(2,1)S(1)}) fusion(pred[5136]{0:T(1024)(128)(4,1)S(1)} %iota_compare_fusion.2, f32[]{:T(128)S(6)} %convert_element_type.47, pred[]{:T(512)S(6)} %lt.50, s32[]{:T(128)S(6)} %select_n.53, s32[128]{0:T(128)} %get-tuple-element.102), kind=kLoop, calls=%fused_computation.9.clone.1 | loop fusion | flops 10518528 | bytes 2635289 | tf_op jit(solution)/shard_map/convert
  798.6 37.6 %select_convert_fusion.3 = (bf16[5136,128]{1,0:T(8,128)(2,1)S(1)}, bf16[5136,128]{1,0:T(8,128)(2,1)S(1)}) fusion(pred[5136]{0:T(1024)(128)(4,1)S(1)} %iota_compare_fusion.2, f32[]{:T(128)S(6)} %convert_element_type.47, pred[]{:T(512)S(6)} %lt.50, s32[]{:T(128)S(6)} %select_n.53, s32[128]{0:T(128)} %get-tuple-element.102), kind=kLoop, calls=%fused_computation.9.clone.1 | loop fusion | flops 10518528 | bytes 2635289 | tf_op jit(solution)/shard_map/convert
  842.4 37.6 %select_convert_fusion.3 = (bf16[5136,128]{1,0:T(8,128)(2,1)S(1)}, bf16[5136,128]{1,0:T(8,128)(2,1)S(1)}) fusion(pred[5136]{0:T(1024)(128)(4,1)S(1)} %iota_compare_fusion.2, f32[]{:T(128)S(6)} %convert_element_type.47, pred[]{:T(512)S(6)} %lt.50, s32[]{:T(128)S(6)} %select_n.53, s32[128]{0:T(128)} %get-tuple-element.102), kind=kLoop, calls=%fused_computation.9.clone.1 | loop fusion | flops 10518528 | bytes 2635289 | tf_op jit(solution)/shard_map/convert
  885.9 12.4 %all-gather.3.cloned.1.call-done = bf16[40,64,2,128]{3,0,2,1:T(8,128)(2,1)} async-done(((bf16[40,32,2,128]{3,0,2,1:T(8,128)(2,1)}), bf16[40,64,2,128]{3,0,2,1:T(8,128)(2,1)}) %all-gather.3.cloned.1.call-update) | async-done | bytes 1310736 | tf_op jit(solution)/shard_map/all_gather | solution.py:57
  913.7 24.2 %all_to_all.18 = bf16[64,2,2560]{2,1,0:T(2,128)(2,1)} all-to-all(bf16[64,2,2560]{2,1,0:T(2,128)(2,1)} %reshape.111), channel_id=1, replica_groups=mesh['lat'=64,'lev'=2] {'lat'}, dimensions={0} | all-to-all | bytes 1310720 | tf_op jit(solution)/shard_map/all_to_all | solution.py:62
  952.9 9.2 all-gather.5.cloned.1.call-done
  (127 shorter events, 140.3 us)
Async XLA Ops:
  6.5 974.0 %copy-start = (bf16[2,2,320,1280]{3,2,1,0:T(8,128)(2,1)S(1)}, bf16[2,2,320,1280]{3,2,1,0:T(8,128)(2,1)}, u32[]{:S(2)}) copy-start(bf16[2,2,320,1280]{3,2,1,0:T(8,128)(2,1)} %param.11) | copy-start | bytes 9830404
  6.5 891.8 %all-gather.3.cloned.1.call-start = ((), (), s32[]{:S(2)}) async-start(), calls=%async_computation.1 | async-start | bytes 1966080 | tf_op jit(solution)/shard_map/all_gather | solution.py:57
  882.4 79.6 %all-gather.5.cloned.1.call-start = ((), (), s32[]{:S(2)}) async-start(), calls=%async_computation.2 | async-start | bytes 1966080 | tf_op jit(solution)/shard_map/all_gather | solution.py:65
  948.0 4.7 copy-start.1
Sparse Core Ops, SparseCore 0:
  882.5 15.7 all-gather.2
  952.8 9.1 all-gather.4
where the time goes:
time: 992 us; the launch traced here: 989 us
  other arithmetic  764 us (77%)
  local copies, waits for them, and re-layouts  88.3 us (9%)
  matrix products  38.9 us (4%)
  loops' own time  38 us (4%)
  blocking collectives  24.2 us (2%)
  waiting for transfers between devices  21.7 us (2%)
  between operations  13.5 us (1%)
    another operation x20, other arithmetic  751 us
    another operation x1, loops' own time, on_device(): lax.map(transform, (grouped, lat_counts))  38 us
    dot_general x20, matrix products, transform(): product = jnp.dot(pair_rows, basis, preferred_element_type=jnp.float32)  34 us
    dynamic_slice x20, local copies, waits for them, and re-layouts, on_device(): lax.map(transform, (grouped, lat_counts))  26.2 us
    all_to_all x1, blocking collectives, on_device(): lax.all_to_all(own_slab.astype(jnp.bfloat16), 'lat', split_axis=0, concat...  24.2 us
  transfers between devices with their start and end apart: 2, of which 2 were waited for; matrix products, arithmetic and copies ran while one was open for 0% of the time, Pallas kernels for 0%

commit v1 on v0

--- a/solution.py
+++ b/solution.py
@@ -59,8 +59,14 @@
     own_slab = lax.dynamic_slice_in_dim(
         mixed_band, lax.axis_index("lev") * slab_width, slab_width, 3
     )
-    slab_owned = lax.all_to_all(
-        own_slab.astype(jnp.bfloat16), "lat", split_axis=0, concat_axis=1, tiled=True
+    slab_owned = jnp.concatenate(
+        lax.all_to_all(
+            jnp.stack(jnp.split(own_slab.astype(jnp.bfloat16), lax.axis_size("lat"), axis=0)),
+            "lat",
+            0,
+            0,
+        ),
+        axis=1,
     ).astype(own_slab.dtype)
     owned = lax.all_gather(slab_owned.astype(jnp.bfloat16), "lev", axis=3, tiled=True).astype(
         slab_owned.dtype

time: 992 us -> 1100 us (1.11)
  local copies, waits for them, and re-layouts: 88.3 us -> 191 us
    unnamed x7 -> x70, local copies, waits for them, and re-layouts: 14.8 us -> 83.6 us
    another operation x0 -> x2, local copies, waits for them, and re-layouts: none -> 39.3 us  [on_device(): jnp.stack(jnp.split(own_slab.astype(jnp.bfloat16), lax.axis_size('lat'),...]
where the time goes in v1:
time: 1100 us; the launch traced here: 1090 us
  other arithmetic  764 us (69%)
  local copies, waits for them, and re-layouts  191 us (17%)
  matrix products  38.9 us (4%)
  loops' own time  38 us (3%)
  blocking collectives  24.4 us (2%)
  waiting for transfers between devices  21.4 us (2%)
  between operations  13.7 us (1%)
    another operation x20, other arithmetic  751 us
    unnamed x70, local copies, waits for them, and re-layouts  83.6 us
    another operation x2, local copies, waits for them, and re-layouts, on_device(): jnp.stack(jnp.split(own_slab.astype(jnp.bfloat16), lax.axis_size('lat'),...  39.3 us
    another operation x1, loops' own time, on_device(): lax.map(transform, (grouped, lat_counts))  38 us
    dot_general x20, matrix products, transform(): product = jnp.dot(pair_rows, basis, preferred_element_type=jnp.float32)  34 us
    dynamic_slice x20, local copies, waits for them, and re-layouts, on_device(): lax.map(transform, (grouped, lat_counts))  26.2 us
    all_to_all x1, blocking collectives, on_device(): lax.all_to_all(jnp.stack(jnp.split(own_slab.astype(jnp.bfloat16), lax.axi...  24.4 us
  transfers between devices with their start and end apart: 2, of which 2 were waited for; matrix products, arithmetic and copies ran while one was open for 0% of the time, Pallas kernels for 0%

profile of v1, /device:TPU:1, one launch (start us, length us, event | category | flops | bytes accessed | tf_op | source)
XLA Modules:
  0.0 1092.7 jit_solution(3769817812661145225)
XLA Ops:
  6.5 875.8 %while.10 = (s32[]{:T(128)}, bf16[20,2,32,2,128]{4,1,0,3,2:T(2,128)(2,1)}, bf16[20,64,5136]{2,1,0:T(8,128)(2,1)}, s32[20]{0:T(128)}, s32[128]{0:T(128)}, /*index=5*/s32[]{:T(128)}, s32[]{:T(128)}) while((s32[]{:T(128)}, bf16[20,2,32,2,128]{4,1,0,3,2:T(2,128)(2,1)}, bf16[20,64,5136]{2,1,0:T(8,128)(2,1)}, s32[20]{0:T(128)}, s32[128]{0:T(128)}, ...), condition=%wide.region_1.2_spmd, body=%wide.region_0.1_spmd.sunk | while | flops 184112144 | bytes 6106801 | solution.py:54
  10.5 37.6 %select_convert_fusion.3 = (bf16[5136,128]{1,0:T(8,128)(2,1)S(1)}, bf16[5136,128]{1,0:T(8,128)(2,1)S(1)}) fusion(pred[5136]{0:T(1024)(128)(4,1)S(1)} %iota_compare_fusion.2, f32[]{:T(128)S(6)} %convert_element_type.47, pred[]{:T(512)S(6)} %lt.50, s32[]{:T(128)S(6)} %select_n.53, s32[128]{0:T(128)} %get-tuple-element.102), kind=kLoop, calls=%fused_computation.9.clone.1 | loop fusion | flops 10518528 | bytes 2635289 | tf_op jit(solution)/shard_map/convert
  54.3 37.6 %select_convert_fusion.3 = (bf16[5136,128]{1,0:T(8,128)(2,1)S(1)}, bf16[5136,128]{1,0:T(8,128)(2,1)S(1)}) fusion(pred[5136]{0:T(1024)(128)(4,1)S(1)} %iota_compare_fusion.2, f32[]{:T(128)S(6)} %convert_element_type.47, pred[]{:T(512)S(6)} %lt.50, s32[]{:T(128)S(6)} %select_n.53, s32[128]{0:T(128)} %get-tuple-element.102), kind=kLoop, calls=%fused_computation.9.clone.1 | loop fusion | flops 10518528 | bytes 2635289 | tf_op jit(solution)/shard_map/convert
  98.1 37.6 %select_convert_fusion.3 = (bf16[5136,128]{1,0:T(8,128)(2,1)S(1)}, bf16[5136,128]{1,0:T(8,128)(2,1)S(1)}) fusion(pred[5136]{0:T(1024)(128)(4,1)S(1)} %iota_compare_fusion.2, f32[]{:T(128)S(6)} %convert_element_type.47, pred[]{:T(512)S(6)} %lt.50, s32[]{:T(128)S(6)} %select_n.53, s32[128]{0:T(128)} %get-tuple-element.102), kind=kLoop, calls=%fused_computation.9.clone.1 | loop fusion | flops 10518528 | bytes 2635289 | tf_op jit(solution)/shard_map/convert
  141.9 37.6 %select_convert_fusion.3 = (bf16[5136,128]{1,0:T(8,128)(2,1)S(1)}, bf16[5136,128]{1,0:T(8,128)(2,1)S(1)}) fusion(pred[5136]{0:T(1024)(128)(4,1)S(1)} %iota_compare_fusion.2, f32[]{:T(128)S(6)} %convert_element_type.47, pred[]{:T(512)S(6)} %lt.50, s32[]{:T(128)S(6)} %select_n.53, s32[128]{0:T(128)} %get-tuple-element.102), kind=kLoop, calls=%fused_computation.9.clone.1 | loop fusion | flops 10518528 | bytes 2635289 | tf_op jit(solution)/shard_map/convert
  185.6 37.6 %select_convert_fusion.3 = (bf16[5136,128]{1,0:T(8,128)(2,1)S(1)}, bf16[5136,128]{1,0:T(8,128)(2,1)S(1)}) fusion(pred[5136]{0:T(1024)(128)(4,1)S(1)} %iota_compare_fusion.2, f32[]{:T(128)S(6)} %convert_element_type.47, pred[]{:T(512)S(6)} %lt.50, s32[]{:T(128)S(6)} %select_n.53, s32[128]{0:T(128)} %get-tuple-element.102), kind=kLoop, calls=%fused_computation.9.clone.1 | loop fusion | flops 10518528 | bytes 2635289 | tf_op jit(solution)/shard_map/convert
  229.4 37.6 %select_convert_fusion.3 = (bf16[5136,128]{1,0:T(8,128)(2,1)S(1)}, bf16[5136,128]{1,0:T(8,128)(2,1)S(1)}) fusion(pred[5136]{0:T(1024)(128)(4,1)S(1)} %iota_compare_fusion.2, f32[]{:T(128)S(6)} %convert_element_type.47, pred[]{:T(512)S(6)} %lt.50, s32[]{:T(128)S(6)} %select_n.53, s32[128]{0:T(128)} %get-tuple-element.102), kind=kLoop, calls=%fused_computation.9.clone.1 | loop fusion | flops 10518528 | bytes 2635289 | tf_op jit(solution)/shard_map/convert
  273.2 37.6 %select_convert_fusion.3 = (bf16[5136,128]{1,0:T(8,128)(2,1)S(1)}, bf16[5136,128]{1,0:T(8,128)(2,1)S(1)}) fusion(pred[5136]{0:T(1024)(128)(4,1)S(1)} %iota_compare_fusion.2, f32[]{:T(128)S(6)} %convert_element_type.47, pred[]{:T(512)S(6)} %lt.50, s32[]{:T(128)S(6)} %select_n.53, s32[128]{0:T(128)} %get-tuple-element.102), kind=kLoop, calls=%fused_computation.9.clone.1 | loop fusion | flops 10518528 | bytes 2635289 | tf_op jit(solution)/shard_map/convert
  317.0 37.6 %select_convert_fusion.3 = (bf16[5136,128]{1,0:T(8,128)(2,1)S(1)}, bf16[5136,128]{1,0:T(8,128)(2,1)S(1)}) fusion(pred[5136]{0:T(1024)(128)(4,1)S(1)} %iota_compare_fusion.2, f32[]{:T(128)S(6)} %convert_element_type.47, pred[]{:T(512)S(6)} %lt.50, s32[]{:T(128)S(6)} %select_n.53, s32[128]{0:T(128)} %get-tuple-element.102), kind=kLoop, calls=%fused_computation.9.clone.1 | loop fusion | flops 10518528 | bytes 2635289 | tf_op jit(solution)/shard_map/convert
  360.7 37.6 %select_convert_fusion.3 = (bf16[5136,128]{1,0:T(8,128)(2,1)S(1)}, bf16[5136,128]{1,0:T(8,128)(2,1)S(1)}) fusion(pred[5136]{0:T(1024)(128)(4,1)S(1)} %iota_compare_fusion.2, f32[]{:T(128)S(6)} %convert_element_type.47, pred[]{:T(512)S(6)} %lt.50, s32[]{:T(128)S(6)} %select_n.53, s32[128]{0:T(128)} %get-tuple-element.102), kind=kLoop, calls=%fused_computation.9.clone.1 | loop fusion | flops 10518528 | bytes 2635289 | tf_op jit(solution)/shard_map/convert
  404.5 37.6 %select_convert_fusion.3 = (bf16[5136,128]{1,0:T(8,128)(2,1)S(1)}, bf16[5136,128]{1,0:T(8,128)(2,1)S(1)}) fusion(pred[5136]{0:T(1024)(128)(4,1)S(1)} %iota_compare_fusion.2, f32[]{:T(128)S(6)} %convert_element_type.47, pred[]{:T(512)S(6)} %lt.50, s32[]{:T(128)S(6)} %select_n.53, s32[128]{0:T(128)} %get-tuple-element.102), kind=kLoop, calls=%fused_computation.9.clone.1 | loop fusion | flops 10518528 | bytes 2635289 | tf_op jit(solution)/shard_map/convert
  448.3 37.6 %select_convert_fusion.3 = (bf16[5136,128]{1,0:T(8,128)(2,1)S(1)}, bf16[5136,128]{1,0:T(8,128)(2,1)S(1)}) fusion(pred[5136]{0:T(1024)(128)(4,1)S(1)} %iota_compare_fusion.2, f32[]{:T(128)S(6)} %convert_element_type.47, pred[]{:T(512)S(6)} %lt.50, s32[]{:T(128)S(6)} %select_n.53, s32[128]{0:T(128)} %get-tuple-element.102), kind=kLoop, calls=%fused_computation.9.clone.1 | loop fusion | flops 10518528 | bytes 2635289 | tf_op jit(solution)/shard_map/convert
  492.1 37.6 %select_convert_fusion.3 = (bf16[5136,128]{1,0:T(8,128)(2,1)S(1)}, bf16[5136,128]{1,0:T(8,128)(2,1)S(1)}) fusion(pred[5136]{0:T(1024)(128)(4,1)S(1)} %iota_compare_fusion.2, f32[]{:T(128)S(6)} %convert_element_type.47, pred[]{:T(512)S(6)} %lt.50, s32[]{:T(128)S(6)} %select_n.53, s32[128]{0:T(128)} %get-tuple-element.102), kind=kLoop, calls=%fused_computation.9.clone.1 | loop fusion | flops 10518528 | bytes 2635289 | tf_op jit(solution)/shard_map/convert
  535.9 37.6 %select_convert_fusion.3 = (bf16[5136,128]{1,0:T(8,128)(2,1)S(1)}, bf16[5136,128]{1,0:T(8,128)(2,1)S(1)}) fusion(pred[5136]{0:T(1024)(128)(4,1)S(1)} %iota_compare_fusion.2, f32[]{:T(128)S(6)} %convert_element_type.47, pred[]{:T(512)S(6)} %lt.50, s32[]{:T(128)S(6)} %select_n.53, s32[128]{0:T(128)} %get-tuple-element.102), kind=kLoop, calls=%fused_computation.9.clone.1 | loop fusion | flops 10518528 | bytes 2635289 | tf_op jit(solution)/shard_map/convert
  579.7 37.6 %select_convert_fusion.3 = (bf16[5136,128]{1,0:T(8,128)(2,1)S(1)}, bf16[5136,128]{1,0:T(8,128)(2,1)S(1)}) fusion(pred[5136]{0:T(1024)(128)(4,1)S(1)} %iota_compare_fusion.2, f32[]{:T(128)S(6)} %convert_element_type.47, pred[]{:T(512)S(6)} %lt.50, s32[]{:T(128)S(6)} %select_n.53, s32[128]{0:T(128)} %get-tuple-element.102), kind=kLoop, calls=%fused_computation.9.clone.1 | loop fusion | flops 10518528 | bytes 2635289 | tf_op jit(solution)/shard_map/convert
  623.5 37.6 %select_convert_fusion.3 = (bf16[5136,128]{1,0:T(8,128)(2,1)S(1)}, bf16[5136,128]{1,0:T(8,128)(2,1)S(1)}) fusion(pred[5136]{0:T(1024)(128)(4,1)S(1)} %iota_compare_fusion.2, f32[]{:T(128)S(6)} %convert_element_type.47, pred[]{:T(512)S(6)} %lt.50, s32[]{:T(128)S(6)} %select_n.53, s32[128]{0:T(128)} %get-tuple-element.102), kind=kLoop, calls=%fused_computation.9.clone.1 | loop fusion | flops 10518528 | bytes 2635289 | tf_op jit(solution)/shard_map/convert
  667.3 37.6 %select_convert_fusion.3 = (bf16[5136,128]{1,0:T(8,128)(2,1)S(1)}, bf16[5136,128]{1,0:T(8,128)(2,1)S(1)}) fusion(pred[5136]{0:T(1024)(128)(4,1)S(1)} %iota_compare_fusion.2, f32[]{:T(128)S(6)} %convert_element_type.47, pred[]{:T(512)S(6)} %lt.50, s32[]{:T(128)S(6)} %select_n.53, s32[128]{0:T(128)} %get-tuple-element.102), kind=kLoop, calls=%fused_computation.9.clone.1 | loop fusion | flops 10518528 | bytes 2635289 | tf_op jit(solution)/shard_map/convert
  711.1 37.6 %select_convert_fusion.3 = (bf16[5136,128]{1,0:T(8,128)(2,1)S(1)}, bf16[5136,128]{1,0:T(8,128)(2,1)S(1)}) fusion(pred[5136]{0:T(1024)(128)(4,1)S(1)} %iota_compare_fusion.2, f32[]{:T(128)S(6)} %convert_element_type.47, pred[]{:T(512)S(6)} %lt.50, s32[]{:T(128)S(6)} %select_n.53, s32[128]{0:T(128)} %get-tuple-element.102), kind=kLoop, calls=%fused_computation.9.clone.1 | loop fusion | flops 10518528 | bytes 2635289 | tf_op jit(solution)/shard_map/convert
  754.8 37.6 %select_convert_fusion.3 = (bf16[5136,128]{1,0:T(8,128)(2,1)S(1)}, bf16[5136,128]{1,0:T(8,128)(2,1)S(1)}) fusion(pred[5136]{0:T(1024)(128)(4,1)S(1)} %iota_compare_fusion.2, f32[]{:T(128)S(6)} %convert_element_type.47, pred[]{:T(512)S(6)} %lt.50, s32[]{:T(128)S(6)} %select_n.53, s32[128]{0:T(128)} %get-tuple-element.102), kind=kLoop, calls=%fused_computation.9.clone.1 | loop fusion | flops 10518528 | bytes 2635289 | tf_op jit(solution)/shard_map/convert
  798.6 37.6 %select_convert_fusion.3 = (bf16[5136,128]{1,0:T(8,128)(2,1)S(1)}, bf16[5136,128]{1,0:T(8,128)(2,1)S(1)}) fusion(pred[5136]{0:T(1024)(128)(4,1)S(1)} %iota_compare_fusion.2, f32[]{:T(128)S(6)} %convert_element_type.47, pred[]{:T(512)S(6)} %lt.50, s32[]{:T(128)S(6)} %select_n.53, s32[128]{0:T(128)} %get-tuple-element.102), kind=kLoop, calls=%fused_computation.9.clone.1 | loop fusion | flops 10518528 | bytes 2635289 | tf_op jit(solution)/shard_map/convert
  842.4 37.6 %select_convert_fusion.3 = (bf16[5136,128]{1,0:T(8,128)(2,1)S(1)}, bf16[5136,128]{1,0:T(8,128)(2,1)S(1)}) fusion(pred[5136]{0:T(1024)(128)(4,1)S(1)} %iota_compare_fusion.2, f32[]{:T(128)S(6)} %convert_element_type.47, pred[]{:T(512)S(6)} %lt.50, s32[]{:T(128)S(6)} %select_n.53, s32[128]{0:T(128)} %get-tuple-element.102), kind=kLoop, calls=%fused_computation.9.clone.1 | loop fusion | flops 10518528 | bytes 2635289 | tf_op jit(solution)/shard_map/convert
  886.2 12.2 %all-gather.3.cloned.1.call-done = bf16[40,64,2,128]{3,0,2,1:T(8,128)(2,1)} async-done(((bf16[40,32,2,128]{3,0,2,1:T(8,128)(2,1)}), bf16[40,64,2,128]{3,0,2,1:T(8,128)(2,1)}) %all-gather.3.cloned.1.call-update) | async-done | bytes 1310736 | tf_op jit(solution)/shard_map/all_gather | solution.py:57
  972.4 38.2 %copy.95 = bf16[64,2,40,2,32]{2,4,3,1,0:T(8,128)(2,1)} copy(bf16[64,2,40,2,32]{1,2,4,3,0:T(8,128)(2,1)} %fusion.37) | data formatting | bytes 1310720 | tf_op jit(solution)/shard_map/stack | solution.py:64
  1016.3 24.4 %all_to_all.5 = bf16[64,2,2560]{2,1,0:T(2,128)(2,1)} all-to-all(bf16[64,2,2560]{2,1,0:T(2,128)(2,1)} %reshape.119), channel_id=1, replica_groups=mesh['lat'=64,'lev'=2] {'lat'}, dimensions={0} | all-to-all | bytes 1310720 | tf_op jit(solution)/shard_map/all_to_all | solution.py:63
  (192 shorter events, 214.6 us)
Async XLA Ops:
  6.5 1077.3 %copy-start = (bf16[2,2,320,1280]{3,2,1,0:T(8,128)(2,1)S(1)}, bf16[2,2,320,1280]{3,2,1,0:T(8,128)(2,1)}, u32[]{:S(2)}) copy-start(bf16[2,2,320,1280]{3,2,1,0:T(8,128)(2,1)} %param.11) | copy-start | bytes 9830404
  6.5 891.8 %all-gather.3.cloned.1.call-start = ((), (), s32[]{:S(2)}) async-start(), calls=%async_computation.1 | async-start | bytes 1966080 | tf_op jit(solution)/shard_map/all_gather | solution.py:57
  882.4 182.9 %all-gather.5.cloned.1.call-start = ((), (), s32[]{:S(2)}) async-start(), calls=%async_computation.2 | async-start | bytes 1966080 | tf_op jit(solution)/shard_map/all_gather | solution.py:71
  954.9 101.1 %copy-start.1 = (s32[128]{0:T(128)S(1)}, s32[128]{0:T(128)}, u32[]{:S(2)}) copy-start(s32[128]{0:T(128)} %get-tuple-element.113) | copy-start | bytes 1540
Sparse Core Ops, SparseCore 0:
  882.5 15.7 all-gather.2
  1056.1 9.1 all-gather.4
